TPU v7x, 32 devices: a whole 2x2x4 slice. The times are simulated.
32 devices in a mesh: grp: 4 (over z), dev: 8 (over y, x, core).
Axes of the slice: x: 2, y: 2, z: 4, core: 2. Of those that a mesh axis runs over, the one named last changes fastest.
Arguments:
- ssm_input: bfloat16 [1024, 4096], P('grp', 'dev'), may hold values from -6 to 6
- gate_input: bfloat16 [1024, 4096], P('grp', 'dev'), may hold values from -6 to 6
- step_size: float32 [1024, 64], P('grp', 'dev'), may hold values from 0.00024414062 to 0.3375
- decay_rate: float32 [64], P('dev'), may hold values from 0.5 to 2
- in_coeff: bfloat16 [1024, 128], P('grp'), may hold values from -6 to 6
- out_coeff: bfloat16 [1024, 128], P('grp'), may hold values from -6 to 6
- skip_gain: float32 [64], P('dev'), may hold values from 0.5 to 3
- norm_gain: float32 [4096], P('dev'), may hold values from 0.5 to 1.5
- out_proj: bfloat16 [4096, 2048], P(None, 'dev'), may hold values from -0.09375 to 0.09375
- residual: bfloat16 [1024, 2048], P(('grp', 'dev')), may hold values from -6 to 6
- ffn_gain: float32 [2048], replicated, may hold values from 0.5 to 1.5
- router: float32 [2048, 4], replicated, may hold values from -0.125 to 0.125
- routes: int32 [1024, 2], P(('grp', 'dev')), may hold values from 0 to 3, all different within a row; in each aligned block of 32 rows (0 to 31, 32 to 63, ...) at most 32 rows name the same one
- gate_weight: bfloat16 [4, 2048, 8192], P('grp', None, 'dev'), may hold values from -0.125 to 0.125
- up_weight: bfloat16 [4, 2048, 8192], P('grp', None, 'dev'), may hold values from -0.125 to 0.125
- down_weight: bfloat16 [4, 8192, 2048], P('grp', 'dev'), may hold values from -0.0625 to 0.0625
Outputs:
- moe_out: bfloat16 [1024, 2048], P(('grp', 'dev'))
Inputs may be any that keep to these rules, and one draw needn't show every extreme that they name: `routes`: each row names two different experts; among the 32 rows of one dispatch block of consecutive tokens no expert is named more than 32 times, a bound that some block reaches.
All inputs are finite; a program needn't handle non-finite values.
Results may differ from a plain program's by a relative error of at most 0.012.
Values may be sent and summed in bfloat16 or wider, within the bound.
A program may use at most 64 MiB of HBM per device.

v0:
```python
import jax
import jax.numpy as jnp
from jax import lax
from jax.sharding import PartitionSpec as P

EPSILON = 1e-05
HIGHEST_PREC = lax.Precision.HIGHEST


def rms_scale(values, gain_vec):
    return (
        values * lax.rsqrt(jnp.mean(values * values, axis=-1, keepdims=True) + EPSILON) * gain_vec
    )


def slot_tables(routes_block, expert_count, slot_cap):
    blocks, row_total = (routes_block.shape[0], routes_block.shape[1])
    flat_routes = routes_block.reshape(blocks, row_total * 2)
    onehot = (
        flat_routes[:, :, None] == jnp.arange(expert_count, dtype=jnp.int32)[None, None, :]
    ).astype(jnp.int32)
    earlier = jnp.cumsum(onehot, axis=1) - onehot
    slot_rank = jnp.sum(earlier * onehot, axis=2)
    slot_index = (flat_routes * slot_cap + slot_rank).reshape(blocks, row_total, 2)
    placed = (
        slot_index[:, :, :, None]
        == jnp.arange(expert_count * slot_cap, dtype=jnp.int32)[None, None, None, :]
    )
    return placed.astype(jnp.float32)


def shards(
    ssm_input,
    gate_input,
    step_size,
    decay_rate,
    in_coeff,
    out_coeff,
    skip_gain,
    norm_gain,
    out_proj,
    residual,
    ffn_gain,
    router,
    routes,
    gate_weight,
    up_weight,
    down_weight,
):
    tok_rows = ssm_input.shape[0]
    head_count = step_size.shape[1]
    head_width = ssm_input.shape[1] // head_count
    dev_count = lax.axis_size("dev")
    inner_dim = ssm_input.shape[1] * dev_count
    block_rows = residual.shape[0]
    model_dim = residual.shape[1]
    experts = lax.axis_size("grp")
    slot_cap = max(2, 4 * block_rows // experts)
    group_slots = experts * slot_cap
    inputs_f = ssm_input.astype(jnp.float32).reshape(tok_rows, head_count, head_width)
    in_float = in_coeff.astype(jnp.float32)
    out_float = out_coeff.astype(jnp.float32)
    log_rate = -(step_size * decay_rate[None, :])
    cumulative = jnp.cumsum(log_rate, axis=0)
    causal = (jnp.arange(tok_rows)[:, None] >= jnp.arange(tok_rows)[None, :])[:, :, None]
    spread = cumulative[:, None, :] - cumulative[None, :, :]
    decay_pair = jnp.where(causal, jnp.exp(jnp.where(causal, spread, 0.0)), 0.0)
    scores = jnp.dot(out_coeff, in_coeff.T, preferred_element_type=jnp.float32)
    mixing = decay_pair * scores[:, :, None] * step_size[None, :, :]
    inside = jnp.einsum("tuh,uhp->thp", mixing, inputs_f, precision=HIGHEST_PREC)
    to_end = jnp.exp(cumulative[-1][None, :] - cumulative) * step_size
    own_state = jnp.einsum("uh,uhp,un->hpn", to_end, inputs_f, in_float, precision=HIGHEST_PREC)
    own_log = cumulative[-1]
    group_logs, group_states = (
        lax.all_gather(own_log[None].astype(jnp.bfloat16), "grp", axis=0, tiled=True).astype(
            jnp.float32
        ),
        lax.all_gather(own_state[None].astype(jnp.bfloat16), "grp", axis=0, tiled=True).astype(
            jnp.float32
        ),
    )
    group_index = jnp.arange(group_logs.shape[0])
    my_group = lax.axis_index("grp")
    inclusive = jnp.cumsum(group_logs, axis=0)
    exclusive = inclusive - group_logs
    before_me = jnp.sum(jnp.where((group_index == my_group)[:, None], exclusive, 0.0), axis=0)
    earlier_mask = (group_index < my_group)[:, None]
    weighting = jnp.where(
        earlier_mask, jnp.exp(jnp.where(earlier_mask, before_me[None, :] - inclusive, 0.0)), 0.0
    )
    entering = jnp.einsum("gh,ghpn->hpn", weighting, group_states, precision=HIGHEST_PREC)
    carried = jnp.exp(cumulative)[:, :, None] * jnp.einsum(
        "hpn,tn->thp", entering, out_float, precision=HIGHEST_PREC
    )
    ssm_out = inside + carried + skip_gain[None, :, None] * inputs_f
    gated_out = ssm_out.reshape(tok_rows, head_count * head_width) * jax.nn.silu(
        gate_input.astype(jnp.float32)
    )
    squares = lax.psum(jnp.sum(gated_out * gated_out, axis=1), "dev")
    mixed_rows = (
        gated_out * lax.rsqrt(squares[:, None] / inner_dim + EPSILON) * norm_gain[None, :]
    ).astype(jnp.bfloat16)
    projected = jnp.dot(
        lax.all_gather(mixed_rows, "dev", axis=1, tiled=True),
        out_proj,
        preferred_element_type=jnp.float32,
    ).astype(jnp.bfloat16)
    mamba_out = lax.all_to_all(projected, "dev", split_axis=0, concat_axis=1, tiled=True)
    hidden_res = (residual.astype(jnp.float32) + mamba_out.astype(jnp.float32)).astype(jnp.bfloat16)
    hidden_float = hidden_res.astype(jnp.float32)
    normed = rms_scale(hidden_float, ffn_gain).astype(jnp.bfloat16)
    logits = jnp.dot(normed.astype(jnp.float32), router, precision=HIGHEST_PREC)
    expert_ids = jnp.arange(experts, dtype=jnp.int32)[None, :]
    first_logit = jnp.sum(logits * (routes[:, 0:1] == expert_ids).astype(jnp.float32), axis=1)
    second_logit = jnp.sum(logits * (routes[:, 1:2] == expert_ids).astype(jnp.float32), axis=1)
    first_prob = jax.nn.sigmoid(first_logit - second_logit)
    second_prob = 1.0 - first_prob
    placed = slot_tables(routes[None], experts, slot_cap)[0]
    filled = jnp.sum(placed, axis=1)
    outgoing = jnp.dot(
        filled.T.astype(jnp.bfloat16), normed, preferred_element_type=jnp.float32
    ).astype(jnp.bfloat16)
    outgoing = outgoing.reshape(experts, slot_cap, model_dim)
    arrived = lax.all_to_all(outgoing, "grp", split_axis=0, concat_axis=0, tiled=True)
    all_rows = lax.all_gather(arrived, "dev", axis=0, tiled=True).reshape(-1, model_dim)
    gate_act = jnp.dot(all_rows, gate_weight[0], preferred_element_type=jnp.float32)
    up_act = jnp.dot(all_rows, up_weight[0], preferred_element_type=jnp.float32)
    hidden = (jax.nn.silu(gate_act) * up_act).astype(jnp.bfloat16)
    summed = lax.psum_scatter(
        jnp.dot(hidden, down_weight[0], preferred_element_type=jnp.float32).astype(jnp.bfloat16),
        "dev",
        scatter_dimension=0,
        tiled=True,
    )
    returned = lax.all_to_all(
        summed.reshape(experts, slot_cap, model_dim), "grp", split_axis=0, concat_axis=0, tiled=True
    )
    weights = first_prob[:, None] * placed[:, 0, :] + second_prob[:, None] * placed[:, 1, :]
    contrib = jnp.dot(
        weights,
        returned.reshape(group_slots, model_dim).astype(jnp.float32),
        precision=HIGHEST_PREC,
    )
    return (hidden_float + contrib).astype(jnp.bfloat16)


def solution(mesh):
    placed = (
        P("grp", "dev"),
        P("grp", "dev"),
        P("grp", "dev"),
        P("dev"),
        P("grp", None),
        P("grp", None),
        P("dev"),
        P("dev"),
        P(None, "dev"),
        P(("grp", "dev"), None),
        P(),
        P(),
        P(("grp", "dev"), None),
        P("grp", None, "dev"),
        P("grp", None, "dev"),
        P("grp", "dev", None),
    )
    return jax.shard_map(
        shards, mesh=mesh, in_specs=placed, out_specs=P(("grp", "dev"), None), check_vma=False
    )
```

profile of v0, /device:TPU:0, one launch (start us, length us, event | category | flops | bytes accessed | tf_op | source)
XLA Modules:
  0.0 247.0 jit_solution(12336162231271233361)
XLA Ops:
  6.6 0.9 negate_bitcast_fusion
  8.7 1.1 copy.42
  9.8 12.6 %all-gather.1 = bf16[4,1,8]{2,1,0:T(2,128)(2,1)S(1)} all-gather(bf16[1,1,8]{2,1,0:T(2,128)(2,1)S(1)} %bitcast.88), channel_id=1, replica_groups=mesh['grp'=4,'dev'=8] {'grp'}, dimensions={0}, use_global_device_ids=true | all-gather | bytes 80 | tf_op jit(solution)/shard_map/all_gather | solution.py:75
  23.3 0.8 exponential_multiply_fusion
  24.1 1.1 fusion.58
  25.1 1.2 convolution_convert_fusion.1
  26.4 14.8 %all-gather = bf16[32,64,128]{2,1,0:T(8,128)(2,1)S(1)} all-gather(bf16[8,64,128]{2,1,0:T(8,128)(2,1)S(1)} %convolution_convert_fusion.1), channel_id=2, replica_groups=mesh['grp'=4,'dev'=8] {'grp'}, dimensions={0}, use_global_device_ids=true | all-gather | bytes 655360 | tf_op jit(solution)/shard_map/all_gather | solution.py:78
  41.2 2.5 %fusion.19 = f32[256,8,64]{0,2,1:T(8,128)S(1)} fusion(bf16[256,8,64]{0,2,1:T(8,128)(2,1)S(1)} %bitcast.77, f32[256,8]{0,1:T(8,128)} %param.18, f32[256,256]{1,0:T(8,128)S(1)} %fusion.58, f32[256,8]{0,1:T(8,128)S(1)} %get-tuple-element.12, pred[256,256]{1,0:T(8,128)(4,1)S(1)} %iota_compare_fusion), kind=kOutput, calls=%fused_computation.18 | convolution fusion | flops 405274624 | bytes 1130496 | tf_op jit(solution)/shard_map/tuh,uhp->thp/dot_general | solution.py:70
  43.7 1.0 fusion.35
  45.7 11.8 %psum.7 = f32[256]{0:T(256)S(1)} all-reduce(f32[256]{0:T(256)S(1)} %multiply_reduce_fusion), channel_id=1, replica_groups=mesh['grp'=4,'dev'=8] {'dev'}, use_global_device_ids=true, to_apply=%region_5.6 | all-reduce | flops 256 | bytes 2048 | tf_op jit(solution)/shard_map/psum | solution.py:99
  57.5 0.9 multiply_convert_fusion.1
  59.2 25.1 %all-gather.5.cloned.1.call-done = bf16[256,4096]{1,0:T(8,128)(2,1)} async-done(((bf16[256,512]{1,0:T(8,128)(2,1)}), bf16[256,4096]{1,0:T(8,128)(2,1)}) %all-gather.5.cloned.1.call-update) | async-done | bytes 2097168 | tf_op jit(solution)/shard_map/all_gather | solution.py:104
  84.3 3.0 %convolution_convert_fusion.2 = bf16[256,256]{1,0:T(8,128)(2,1)} fusion(bf16[256,4096]{1,0:T(8,128)(2,1)} %all-gather.5.cloned.1.call-done, bf16[4096,256]{1,0:T(8,128)(2,1)S(1)} %copy-done), kind=kOutput, calls=%fused_computation.24 | convolution fusion | flops 536936448 | bytes 4325376 | tf_op jit(solution)/shard_map/dot_general | solution.py:103
  87.2 3.4 %all-to-all-start = ((bf16[8,32,256]{2,1,0:T(8,128)(2,1)}), bf16[8,32,256]{2,1,0:T(8,128)(2,1)S(1)}, u32[]{:S(2)}, u32[]{:S(2)}) async-start(bf16[8,32,256]{2,1,0:T(8,128)(2,1)} %bitcast.16), calls=%async_computation | async-start | bytes 262144 | tf_op jit(solution)/shard_map/all_to_all | solution.py:108
  90.7 5.3 %all-to-all-done = bf16[8,32,256]{2,1,0:T(8,128)(2,1)S(1)} async-done(((bf16[8,32,256]{2,1,0:T(8,128)(2,1)}), bf16[8,32,256]{2,1,0:T(8,128)(2,1)S(1)}, u32[]{:S(2)}, u32[]{:S(2)}) %all-to-all-start) | async-done | bytes 131104 | tf_op jit(solution)/shard_map/all_to_all | solution.py:108
  96.6 18.8 %all_to_all.23 = bf16[4,32,2048]{2,1,0:T(8,128)(2,1)} all-to-all(bf16[4,32,2048]{2,1,0:T(8,128)(2,1)S(1)} %bitcast.81), channel_id=1, replica_groups=mesh['grp'=4,'dev'=8] {'grp'}, dimensions={0} | all-to-all | bytes 1048576 | tf_op jit(solution)/shard_map/all_to_all | solution.py:124
  115.7 34.0 %all-gather.7.cloned.1.call-done = bf16[32,32,2048]{2,1,0:T(8,128)(2,1)} async-done(((bf16[4,32,2048]{2,1,0:T(8,128)(2,1)}), bf16[32,32,2048]{2,1,0:T(8,128)(2,1)}) %all-gather.7.cloned.1.call-update) | async-done | bytes 4194320 | tf_op jit(solution)/shard_map/all_gather | solution.py:125
  149.7 7.6 %fusion.2 = f32[1024,1024]{1,0:T(8,128)S(1)} fusion(bf16[1024,2048]{1,0:T(8,128)(2,1)} %bitcast.89, bf16[1,2048,1024]{2,1,0:T(8,128)(2,1)} %param.30), kind=kOutput, calls=%fused_computation.2 | convolution fusion | flops 4294967296 | bytes 12582912 | tf_op jit(solution)/shard_map/dot_general | solution.py:127
  157.4 5.4 %multiply_convert_fusion = bf16[1024,1024]{1,0:T(8,128)(2,1)S(1)} fusion(f32[1024,1024]{1,0:T(8,128)S(1)} %fusion.2, bf16[1024,2048]{1,0:T(8,128)(2,1)S(1)} %bitcast.90, bf16[1,2048,1024]{2,1,0:T(8,128)(2,1)S(1)} %copy-done.9), kind=kOutput, calls=%fused_computation.6 | convolution fusion | flops 4301258752 | bytes 14680064 | tf_op jit(solution)/shard_map/dot_general | solution.py:126
  162.7 6.1 %fusion.6 = bf16[1024,2048]{1,0:T(8,128)(2,1)} fusion(bf16[1024,1024]{1,0:T(8,128)(2,1)S(1)} %multiply_convert_fusion, bf16[1,1024,2048]{2,1,0:T(8,128)(2,1)S(1)} %copy-done.10), kind=kOutput, calls=%fused_computation.7 | convolution fusion | flops 4297064448 | bytes 10485760 | tf_op jit(solution)/shard_map/dot_general | solution.py:130
  168.8 51.5 %reduce-scatter.2.cloned.1.call-done = bf16[128,2048]{1,0:T(8,128)(2,1)} async-done(((bf16[1024,2048]{1,0:T(8,128)(2,1)}), bf16[128,2048]{1,0:T(8,128)(2,1)}) %reduce-scatter.2.cloned.1.call-update) | async-done | bytes 524304 | tf_op jit(solution)/shard_map/reduce_scatter | solution.py:129
  220.3 4.6 %all-to-all-start.2 = ((bf16[4,32,2048]{2,1,0:T(8,128)(2,1)}), bf16[4,32,2048]{2,1,0:T(8,128)(2,1)S(1)}, u32[]{:S(2)}, u32[]{:S(2)}) async-start(bf16[4,32,2048]{2,1,0:T(8,128)(2,1)} %bitcast.84), calls=%async_computation.3 | async-start | bytes 1048576 | tf_op jit(solution)/shard_map/all_to_all | solution.py:135
  225.3 14.1 %all-to-all-done.2 = bf16[4,32,2048]{2,1,0:T(8,128)(2,1)S(1)} async-done(((bf16[4,32,2048]{2,1,0:T(8,128)(2,1)}), bf16[4,32,2048]{2,1,0:T(8,128)(2,1)S(1)}, u32[]{:S(2)}, u32[]{:S(2)}) %all-to-all-start.2) | async-done | bytes 524320 | tf_op jit(solution)/shard_map/all_to_all | solution.py:135
  239.4 1.1 fusion.11
  (69 shorter events, 5.1 us)
Async XLA Ops:
  6.5 77.7 %copy-start = (bf16[4096,256]{1,0:T(8,128)(2,1)S(1)}, bf16[4096,256]{1,0:T(8,128)(2,1)}, u32[]{:S(2)}) copy-start(bf16[4096,256]{1,0:T(8,128)(2,1)} %param.24) | copy-start | bytes 6291460
  6.5 38.2 %copy-start.2 = (bf16[256,128]{1,0:T(8,128)(2,1)S(1)}, bf16[256,128]{1,0:T(8,128)(2,1)}, u32[]{:S(2)}) copy-start(bf16[256,128]{1,0:T(8,128)(2,1)} %param.21) | copy-start | bytes 196612
  6.5 77.7 %all-gather.5.cloned.1.call-start = ((), (), s32[]{:S(2)}) async-start(), calls=%async_computation.4 | async-start | bytes 2359296 | tf_op jit(solution)/shard_map/all_gather | solution.py:104
  23.3 20.4 %copy-start.6 = (f32[4,8,1,1]{0,2,3,1:T(1,128)S(1)}, f32[4,8,1,1]{0,2,3,1:T(1,128)}, u32[]{:S(2)}) copy-start(f32[4,8,1,1]{0,2,3,1:T(1,128)} %copy.47) | copy-start | bytes 388
  23.3 21.5 %copy-start.8 = (f32[8]{0:T(128)S(1)}, f32[8]{0:T(128)}, u32[]{:S(2)}) copy-start(f32[8]{0:T(128)} %param.22) | copy-start | bytes 100
  41.2 4.2 %copy-start.1 = (bf16[256,512]{1,0:T(8,128)(2,1)S(1)}, bf16[256,512]{1,0:T(8,128)(2,1)}, u32[]{:S(2)}) copy-start(bf16[256,512]{1,0:T(8,128)(2,1)} %param.17) | copy-start | bytes 786436
  43.7 13.8 %copy-start.7 = (f32[512]{0:T(512)S(1)}, f32[512]{0:T(512)}, u32[]{:S(2)}) copy-start(f32[512]{0:T(512)} %param.23) | copy-start | bytes 6148
  43.7 14.7 %copy-start.4 = (s32[32,2]{0,1:T(2,128)S(1)}, s32[32,2]{0,1:T(2,128)}, u32[]{:S(2)}) copy-start(s32[32,2]{0,1:T(2,128)} %param.28) | copy-start | bytes 772
  45.4 50.7 %copy-start.3 = (bf16[32,2048]{1,0:T(8,128)(2,1)S(1)}, bf16[32,2048]{1,0:T(8,128)(2,1)}, u32[]{:S(2)}) copy-start(bf16[32,2048]{1,0:T(8,128)(2,1)} %param.25) | copy-start | bytes 393220
  45.4 50.9 %copy-start.5 = (f32[2048]{0:T(1024)S(1)}, f32[2048]{0:T(1024)}, u32[]{:S(2)}) copy-start(f32[2048]{0:T(1024)} %param.26) | copy-start | bytes 24580
  87.2 8.8 %all-to-all-start = ((bf16[8,32,256]{2,1,0:T(8,128)(2,1)}), bf16[8,32,256]{2,1,0:T(8,128)(2,1)S(1)}, u32[]{:S(2)}, u32[]{:S(2)}) async-start(bf16[8,32,256]{2,1,0:T(8,128)(2,1)} %bitcast.16), calls=%async_computation | async-start | bytes 262144 | tf_op jit(solution)/shard_map/all_to_all | solution.py:108
  90.6 59.1 %all-gather.7.cloned.1.call-start = ((), (), s32[]{:S(2)}) async-start(), calls=%async_computation.5 | async-start | bytes 4718592 | tf_op jit(solution)/shard_map/all_gather | solution.py:125
  115.5 104.9 %reduce-scatter.2.cloned.1.call-start = ((), (), s32[]{:S(2)}) async-start(), calls=%async_computation.6 | async-start | bytes 4718592 | tf_op jit(solution)/shard_map/reduce_scatter | solution.py:129
  149.7 7.7 %copy-start.9 = (bf16[1,2048,1024]{2,1,0:T(8,128)(2,1)S(1)}, bf16[1,2048,1024]{2,1,0:T(8,128)(2,1)}, u32[]{:S(2)}) copy-start(bf16[1,2048,1024]{2,1,0:T(8,128)(2,1)} %param.29) | copy-start | bytes 12582916
  149.7 7.7 %copy-start.11 = (bf16[32,32,2048]{2,1,0:T(8,128)(2,1)S(1)}, bf16[32,32,2048]{2,1,0:T(8,128)(2,1)}, u32[]{:S(2)}) copy-start(bf16[32,32,2048]{2,1,0:T(8,128)(2,1)} %all-gather.7.cloned.1.call-done) | copy-start | bytes 12582916
  157.4 5.4 %copy-start.10 = (bf16[1,1024,2048]{2,1,0:T(8,128)(2,1)S(1)}, bf16[1,1024,2048]{2,1,0:T(8,128)(2,1)}, u32[]{:S(2)}) copy-start(bf16[1,1024,2048]{2,1,0:T(8,128)(2,1)} %param.31) | copy-start | bytes 12582916
  168.8 56.2 %copy-start.12 = (f32[2048,4]{0,1:T(4,128)S(1)}, f32[2048,4]{0,1:T(4,128)}, u32[]{:S(2)}) copy-start(f32[2048,4]{0,1:T(4,128)} %param.27) | copy-start | bytes 98308
  220.3 19.1 %all-to-all-start.2 = ((bf16[4,32,2048]{2,1,0:T(8,128)(2,1)}), bf16[4,32,2048]{2,1,0:T(8,128)(2,1)S(1)}, u32[]{:S(2)}, u32[]{:S(2)}) async-start(bf16[4,32,2048]{2,1,0:T(8,128)(2,1)} %bitcast.84), calls=%async_computation.3 | async-start | bytes 1048576 | tf_op jit(solution)/shard_map/all_to_all | solution.py:135
Sparse Core Ops, SparseCore 0:
  58.6 25.6 all-gather.4
  115.6 34.0 all-gather.6
  169.0 51.3 reduce-scatter.1
where the time goes:
time: 248 us; the launch traced here: 247 us
  waiting for transfers between devices  130 us (52%)
  blocking collectives  58 us (23%)
  matrix products  30 us (12%)
  between operations  13.4 us (5%)
  starting transfers between devices  8.22 us (3%)
  other arithmetic  4.5 us (2%)
  local copies, waits for them, and re-layouts  2.95 us (1%)
    reduce_scatter x1, waiting for transfers between devices, shards(): lax.psum_scatter(jnp.dot(hidden, down_weight[0], preferred_element_type=j...  51.5 us
    all_gather x1, waiting for transfers between devices, shards(): lax.all_gather(arrived, 'dev', axis=0, tiled=True).reshape(-1, model_dim)  34 us
    all_gather x1, waiting for transfers between devices, shards(): lax.all_gather(mixed_rows, 'dev', axis=1, tiled=True)  25.1 us
    all_to_all x1, blocking collectives, shards(): lax.all_to_all(outgoing, 'grp', split_axis=0, concat_axis=0, tiled=True)  18.8 us
    all_gather x1, blocking collectives, shards(): lax.all_gather(own_state[None].astype(jnp.bfloat16), 'grp', axis=0, tiled...  14.8 us
    all_to_all x1, waiting for transfers between devices, shards(): lax.all_to_all(summed.reshape(experts, slot_cap, model_dim), 'grp', split...  14.1 us
    all_gather x1, blocking collectives, shards(): lax.all_gather(own_log[None].astype(jnp.bfloat16), 'grp', axis=0, tiled=T...  12.6 us
    psum x1, blocking collectives, shards(): squares = lax.psum(jnp.sum(gated_out * gated_out, axis=1), 'dev')  11.8 us
  transfers between devices with their start and end apart: 5, of which 5 were waited for; matrix products, arithmetic and copies ran while one was open for 0% of the time, Pallas kernels for 0%

commit v1 on v0

--- a/solution.py
+++ b/solution.py
@@ -1,6 +1,8 @@
 import jax
 import jax.numpy as jnp
 from jax import lax
+from jax.experimental import pallas as pl
+from jax.experimental.pallas import tpu as pltpu
 from jax.sharding import PartitionSpec as P
 
 EPSILON = 1e-05
@@ -19,7 +21,9 @@
     onehot = (
         flat_routes[:, :, None] == jnp.arange(expert_count, dtype=jnp.int32)[None, None, :]
     ).astype(jnp.int32)
-    earlier = jnp.cumsum(onehot, axis=1) - onehot
+    rank = jnp.arange(row_total * 2)
+    before = (rank[:, None] > rank[None, :]).astype(jnp.int32)
+    earlier = jnp.sum(before[None, :, :, None] * onehot[:, None, :, :], axis=2)
     slot_rank = jnp.sum(earlier * onehot, axis=2)
     slot_index = (flat_routes * slot_cap + slot_rank).reshape(blocks, row_total, 2)
     placed = (
@@ -61,7 +65,8 @@
     in_float = in_coeff.astype(jnp.float32)
     out_float = out_coeff.astype(jnp.float32)
     log_rate = -(step_size * decay_rate[None, :])
-    cumulative = jnp.cumsum(log_rate, axis=0)
+    lower = jnp.arange(tok_rows)[:, None] >= jnp.arange(tok_rows)[None, :]
+    cumulative = jnp.dot(lower.astype(jnp.float32), log_rate, precision=HIGHEST_PREC)
     causal = (jnp.arange(tok_rows)[:, None] >= jnp.arange(tok_rows)[None, :])[:, :, None]
     spread = cumulative[:, None, :] - cumulative[None, :, :]
     decay_pair = jnp.where(causal, jnp.exp(jnp.where(causal, spread, 0.0)), 0.0)
@@ -81,7 +86,10 @@
     )
     group_index = jnp.arange(group_logs.shape[0])
     my_group = lax.axis_index("grp")
-    inclusive = jnp.cumsum(group_logs, axis=0)
+    inclusive = jnp.sum(
+        jnp.where((group_index[:, None] >= group_index[None, :])[:, :, None], group_logs[None], 0.0),
+        axis=1,
+    )
     exclusive = inclusive - group_logs
     before_me = jnp.sum(jnp.where((group_index == my_group)[:, None], exclusive, 0.0), axis=0)
     earlier_mask = (group_index < my_group)[:, None]
@@ -144,6 +152,474 @@
     return (hidden_float + contrib).astype(jnp.bfloat16)
 
 
+ACROSS_X, ACROSS_Y, ACROSS_CORE = 1, 2, 4
+GATHER_ORDER = (0, 4, 1, 2, 5, 6, 3, 7)
+BF16, F32 = jnp.bfloat16, jnp.float32
+
+
+def fused_kernel(
+    ssm, gate, step, decay, in_c, out_c, skip, gain, res, ffn, router, routes,
+    wp_hbm, wg_hbm, wu_hbm, wd_hbm,
+    out,
+    wp, wg, wu, wd, own_state, st_in, st_out, y_buf, g_all, ss_send, ss_recv, pr_send, pr_recv,
+    hid, x_all, h_buf, part, core_in, acc, x_in, y_in, mid, y_in2, x_in2, fin, z_in,
+    w_sem, st_s, st_r, ag_s, ag_r, ss_s, ss_r, pr_s, pr_r, zx_s, zx_r, rs_s, rs_r,
+):
+    z, d = lax.axis_index("grp"), lax.axis_index("dev")
+    rows, chans = ssm.shape
+    heads = step.shape[1]
+    width = chans // heads
+    n_state = in_c.shape[1]
+    tok, dim = res.shape
+    half = dim // 2
+    hidden_units = wg.shape[1]
+    cols = wp.shape[1]
+    core0, x0, y0 = lax.rem(d, 2), lax.rem(lax.div(d, 2), 2), lax.div(d, 4)
+
+    def dev_of(r):
+        c = 1 - core0 if r & ACROSS_CORE else core0
+        x = 1 - x0 if r & ACROSS_X else x0
+        y = 1 - y0 if r & ACROSS_Y else y0
+        return (y * 2 + x) * 2 + c
+
+    def grp_of(k):
+        return (z, z + 1 - 2 * lax.rem(z, 2), lax.rem(z + 2, 4), 3 - z)[k]
+
+    sent = []
+
+    def push(src, dst, s_sem, r_sem, to):
+        copy = pltpu.make_async_remote_copy(
+            src_ref=src, dst_ref=dst, send_sem=s_sem, recv_sem=r_sem,
+            device_id=to, device_id_type=pl.DeviceIdType.MESH,
+        )
+        copy.start()
+        sent.append(copy)
+
+    def arrived(dst, s_sem, r_sem, to):
+        pltpu.make_async_remote_copy(
+            src_ref=dst, dst_ref=dst, send_sem=s_sem, recv_sem=r_sem,
+            device_id=to, device_id_type=pl.DeviceIdType.MESH,
+        ).wait_recv()
+
+    loads = [
+        pltpu.make_async_copy(wp_hbm, wp, w_sem.at[0]),
+        pltpu.make_async_copy(wg_hbm.at[0], wg, w_sem.at[1]),
+        pltpu.make_async_copy(wu_hbm.at[0], wu, w_sem.at[2]),
+        pltpu.make_async_copy(wd_hbm.at[0], wd, w_sem.at[3]),
+    ]
+    for load in loads:
+        load.start()
+
+    barrier = pltpu.get_barrier_semaphore()
+    for r in range(1, 8):
+        pl.semaphore_signal(
+            barrier, inc=1, device_id=(z, dev_of(r)), device_id_type=pl.DeviceIdType.MESH
+        )
+    for k in range(1, 4):
+        pl.semaphore_signal(
+            barrier, inc=1, device_id=(grp_of(k), d), device_id_type=pl.DeviceIdType.MESH
+        )
+
+    def iota(shape, axis):
+        return lax.broadcasted_iota(jnp.int32, shape, axis)
+
+    def exact(a, b):
+        return jnp.dot(a, b, precision=HIGHEST_PREC, preferred_element_type=F32)
+
+    causal = iota((rows, rows), 0) >= iota((rows, rows), 1)
+    pad = (iota((heads, 128), 0) == iota((heads, 128), 1)).astype(F32)
+    expand = (iota((128, chans), 0) == lax.div(iota((128, chans), 1), width)).astype(F32)
+    log_pad = exact(-(step[...] * decay[...]), pad)
+    step_pad = exact(step[...], pad)
+    cum = exact(causal.astype(F32), log_pad)
+    cum_t, step_t = cum.T, step_pad.T
+    cum_wide, step_wide = exact(cum, expand), exact(step_pad, expand)
+    last = cum_wide[rows - 1 : rows]
+    xf = ssm[...].astype(F32)
+    weighted = (jnp.exp(last - cum_wide) * step_wide * xf).astype(BF16)
+    in_t = in_c[...].astype(F32).T.astype(BF16)
+    own_state[...] = jnp.dot(in_t, weighted, preferred_element_type=F32)
+    group_decay = jnp.exp(last)
+    pl.semaphore_wait(barrier, 10)
+
+    pieces = st_in.shape[0]
+    pw = chans // pieces
+
+    def state_copy(c):
+        return pltpu.make_async_remote_copy(
+            src_ref=st_out.at[c], dst_ref=st_in.at[c], send_sem=st_s.at[c], recv_sem=st_r.at[c],
+            device_id=(lax.rem(z + 1, 4), d), device_id_type=pl.DeviceIdType.MESH,
+        )
+
+    def relay(c):
+        at = slice(c * pw, (c + 1) * pw)
+        state_copy(c).wait_recv()
+        st_out[c] = (group_decay[:, at] * st_in[c].astype(F32) + own_state[:, at]).astype(BF16)
+        state_copy(c).start()
+
+    @pl.when(z == 0)
+    def _():
+        for c in range(pieces):
+            st_out[c] = own_state[:, c * pw : (c + 1) * pw].astype(BF16)
+            state_copy(c).start()
+        st_in[...] = jnp.zeros_like(st_in)
+
+    scores = lax.dot_general(
+        out_c[...], in_c[...], (((1,), (1,)), ((), ())), preferred_element_type=F32
+    )
+    scores = jnp.where(causal, scores, 0.0)
+    low_lane = iota((rows, 2 * width), 1) < width
+    skip_wide = exact(jnp.broadcast_to(skip[...], (8, heads)), expand[0:heads])[0:1]
+
+    def inside(c):
+        at = slice(c * pw, (c + 1) * pw)
+        x_pair = ssm[:, at]
+        pair = []
+        for h in (2 * c, 2 * c + 1):
+            spread = cum[:, h : h + 1] - cum_t[h : h + 1, :]
+            mixing = jnp.exp(jnp.minimum(spread, 0.0)) * scores * step_t[h : h + 1, :]
+            pair.append(jnp.dot(mixing.astype(BF16), x_pair, preferred_element_type=F32))
+        y_buf[:, at] = jnp.where(low_lane, pair[0], pair[1]) + skip_wide[:, at] * xf[:, at]
+
+    def relay_at(group, first):
+        @pl.when(z == group)
+        def _():
+            for c in (first, first + 1):
+                relay(c)
+
+    inside(0)
+    relay_at(1, 0)
+    inside(1)
+    relay_at(1, 2)
+    relay_at(2, 0)
+    inside(2)
+    relay_at(2, 2)
+    inside(3)
+
+    @pl.when(z == 3)
+    def _():
+        for c in range(pieces):
+            state_copy(c).wait_recv()
+
+    carried = jnp.concatenate(
+        [jnp.dot(out_c[...], st_in[c], preferred_element_type=F32) for c in range(pieces)], axis=1
+    )
+    gf = gate[...].astype(F32)
+    gated = (y_buf[...] + jnp.exp(cum_wide) * carried) * (gf / (1.0 + jnp.exp(-gf)))
+    g_all[0] = (gated * gain[...]).astype(BF16)
+
+    class Gather:
+        def __init__(self, number, ref_at, length):
+            self.n, self.at, self.length = number, ref_at, length
+
+        def hop(self, src, through, lo, size, sem):
+            dst = src ^ through
+            push(
+                self.at(src, lo, size), self.at(dst, lo, size),
+                ag_s.at[self.n, sem], ag_r.at[self.n, sem], (z, dev_of(through)),
+            )
+
+        def wait(self, slot):
+            if slot == 3:
+                h = self.length // 2
+                for lo, sem in ((0, 3), (h, 0)):
+                    arrived(
+                        self.at(3, lo, h), ag_s.at[self.n, sem], ag_r.at[self.n, sem], (z, d)
+                    )
+            else:
+                arrived(
+                    self.at(slot, 0, self.length),
+                    ag_s.at[self.n, slot], ag_r.at[self.n, slot], (z, d),
+                )
+
+        def first(self):
+            self.hop(0, ACROSS_X, 0, self.length, 1)
+            self.hop(0, ACROSS_Y, 0, self.length, 2)
+            self.hop(0, ACROSS_CORE, 0, self.length, 4)
+
+        def second(self):
+            h = self.length // 2
+            self.wait(1)
+            self.hop(1, ACROSS_Y, 0, h, 3)
+            self.hop(1, ACROSS_CORE, 0, self.length, 5)
+            self.wait(2)
+            self.hop(2, ACROSS_X, h, h, 0)
+            self.hop(2, ACROSS_CORE, 0, self.length, 6)
+
+        def third(self):
+            self.wait(3)
+            self.hop(3, ACROSS_CORE, 0, self.length, 7)
+
+        def rest(self):
+            for slot in (4, 5, 6, 7):
+                self.wait(slot)
+
+    mixer = Gather(4, lambda r, lo, size: g_all.at[r, pl.ds(lo, size)], rows)
+    mixer.first()
+    squares = jnp.sum(gated * gated, axis=1, keepdims=True)
+    ss_send[...] = jnp.broadcast_to(squares, ss_send.shape)
+
+    def own_rows(r):
+        return pl.ds(pl.multiple_of(dev_of(r) * tok, tok), tok)
+
+    for r in range(1, 8):
+        push(
+            ss_send.at[own_rows(r)], ss_recv.at[d], ss_s.at[r], ss_r.at[r], (z, dev_of(r))
+        )
+    ss_recv[d] = ss_send[own_rows(0)]
+    loads[0].wait()
+
+    def project(r):
+        w_rows = pl.ds(pl.multiple_of(dev_of(r) * chans, chans), chans)
+        return jnp.dot(g_all[r], wp[w_rows, :], preferred_element_type=F32)
+
+    total = project(0)
+    mixer.second()
+    mixer.wait(4)
+    total = total + project(4)
+    total = total + project(1)
+    mixer.third()
+    total = total + project(2)
+    for r in (5, 6):
+        mixer.wait(r)
+        total = total + project(r)
+    total = total + project(3)
+    mixer.wait(7)
+    total = total + project(7)
+    pr_send[...] = total.astype(BF16)
+    for r in range(1, 8):
+        push(
+            pr_send.at[own_rows(r)], pr_recv.at[d], pr_s.at[r], pr_r.at[r], (z, dev_of(r))
+        )
+    pr_recv[d] = pr_send[own_rows(0)]
+    for r in range(1, 8):
+        arrived(ss_recv.at[dev_of(r)], ss_s.at[r], ss_r.at[r], (z, d))
+    norm = ss_recv[0]
+    for j in range(1, 8):
+        norm = norm + ss_recv[j]
+    norm = lax.rsqrt(norm[:, 0:1] / (chans * 8) + EPSILON)
+    for r in range(1, 8):
+        arrived(pr_recv.at[dev_of(r)], pr_s.at[r], pr_r.at[r], (z, d))
+    square = jnp.zeros((tok, cols), F32)
+    for j in range(8):
+        at = slice(j * cols, (j + 1) * cols)
+        mamba = (pr_recv[j].astype(F32) * norm).astype(BF16).astype(F32)
+        value = (res[:, at].astype(F32) + mamba).astype(BF16).astype(F32)
+        hid[:, at] = value
+        square = square + value * value
+    inv = lax.rsqrt(jnp.sum(square, axis=1, keepdims=True) / dim + EPSILON)
+    x_all[0, 0:tok] = (hid[...] * inv * ffn[...]).astype(BF16)
+
+    for k in (1, 3, 2):
+        push(
+            x_all.at[0, 0:tok], x_all.at[k, 0:tok], zx_s.at[k], zx_r.at[k], (grp_of(k), d)
+        )
+
+    def chunk_view(k):
+        return lambda r, lo, size: x_all.at[k, pl.ds(r * tok + lo, size)]
+
+    gathers = [Gather(k, chunk_view(k), tok) for k in range(4)]
+    turn = (0, 1, 3, 2)
+
+    def gather_first(k):
+        if k > 0:
+            arrived(x_all.at[k, 0:tok], zx_s.at[k], zx_r.at[k], (z, d))
+        gathers[k].first()
+
+    gather_first(0)
+    logits = exact(x_all[0, 0:tok].astype(F32), router[...])
+    experts = logits.shape[1]
+    ids = iota((tok, experts), 1)
+    named0, named1 = routes[:, 0:1] == ids, routes[:, 1:2] == ids
+    logit0 = jnp.sum(jnp.where(named0, logits, 0.0), axis=1, keepdims=True)
+    logit1 = jnp.sum(jnp.where(named1, logits, 0.0), axis=1, keepdims=True)
+    prob0 = 1.0 / (1.0 + jnp.exp(-(logit0 - logit1)))
+    prob1 = 1.0 - prob0
+
+    def expert_weight(e):
+        return jnp.where(routes[:, 0:1] == e, prob0, 0.0) + jnp.where(
+            routes[:, 1:2] == e, prob1, 0.0
+        )
+
+    gathers[0].second()
+    gather_first(turn[1])
+    gathers[0].third()
+    for load in loads[1:]:
+        load.wait()
+    gathers[0].rest()
+    tile = 256
+    lower, upper = slice(0, half), slice(half, dim)
+    core_rows = slice(4 * tok, 8 * tok)
+
+    def gate_up(k, begin, end):
+        @pl.loop(begin, end)
+        def _(i):
+            at = pl.ds(pl.multiple_of(i * tile, tile), tile)
+            x = x_all[k]
+            g = jnp.dot(x, wg[:, at], preferred_element_type=F32)
+            u = jnp.dot(x, wu[:, at], preferred_element_type=F32)
+            h_buf[:, at] = (g / (1.0 + jnp.exp(-g)) * u).astype(BF16)
+
+    def down(k, begin, end):
+        @pl.loop(begin, end)
+        def _(i):
+            at = pl.ds(pl.multiple_of(i * tile, tile), tile)
+            part[k, :, at] = jnp.dot(
+                h_buf[...], wd[:, at], preferred_element_type=F32
+            ).astype(BF16)
+
+    def rs_push(k, n, src, dst, through):
+        push(src, dst, rs_s.at[k, n], rs_r.at[k, n], (z, dev_of(through)))
+
+    def rs_wait(k, n, dst):
+        arrived(dst, rs_s.at[k, n], rs_r.at[k, n], (z, d))
+
+    def add(a, b):
+        return (a.astype(F32) + b.astype(F32)).astype(BF16)
+
+    def core_send(k, n):
+        at = (lower, upper)[n]
+        rs_push(k, n, part.at[k, core_rows, at], core_in.at[k, :, at], ACROSS_CORE)
+
+    def reduce_first(k):
+        rs_wait(k, 0, core_in.at[k, :, lower])
+        acc[k, :, lower] = add(part[k, 0 : 4 * tok, lower], core_in[k, :, lower])
+        rs_push(k, 2, acc.at[k, tok : 2 * tok, lower], x_in.at[k, 0:tok], ACROSS_X)
+        rs_push(k, 3, acc.at[k, 3 * tok : 4 * tok, lower], x_in.at[k, tok : 2 * tok], ACROSS_X)
+        rs_wait(k, 1, core_in.at[k, :, upper])
+        acc[k, :, upper] = add(part[k, 0 : 4 * tok, upper], core_in[k, :, upper])
+        rs_push(k, 4, acc.at[k, 2 * tok : 4 * tok, upper], y_in.at[k], ACROSS_Y)
+
+    def reduce_second(k):
+        rs_wait(k, 2, x_in.at[k, 0:tok])
+        rs_wait(k, 3, x_in.at[k, tok : 2 * tok])
+        mid[k, 0] = add(acc[k, 2 * tok : 3 * tok, lower], x_in[k, tok : 2 * tok])
+        rs_push(k, 5, mid.at[k, 0], y_in2.at[k], ACROSS_Y)
+        rs_wait(k, 4, y_in.at[k])
+        mid[k, 1] = add(acc[k, tok : 2 * tok, upper], y_in[k, tok : 2 * tok])
+        rs_push(k, 6, mid.at[k, 1], x_in2.at[k], ACROSS_X)
+
+    def reduce_third(k):
+        near_x = acc[k, 0:tok, lower].astype(F32) + x_in[k, 0:tok].astype(F32)
+        near_y = acc[k, 0:tok, upper].astype(F32) + y_in[k, 0:tok].astype(F32)
+        rs_wait(k, 5, y_in2.at[k])
+        fin[k, :, lower] = add(near_x, y_in2[k])
+        rs_wait(k, 6, x_in2.at[k])
+        fin[k, :, upper] = add(near_y, x_in2[k])
+        if k > 0:
+            push(fin.at[k], z_in.at[k], rs_s.at[k, 7], rs_r.at[k, 7], (grp_of(k), d))
+
+    gu, dn = hidden_units // tile, dim // tile
+    for n in range(4):
+        k = turn[n]
+        before = turn[n - 1] if n > 0 else None
+        after = turn[n + 1] if n < 3 else None
+        if n > 0:
+            gathers[k].rest()
+        gate_up(k, 0, gu // 2)
+        if after is not None:
+            gathers[after].second()
+        if n < 2:
+            gather_first(turn[n + 2])
+        if before is not None:
+            reduce_first(before)
+        gate_up(k, gu // 2, gu)
+        if after is not None:
+            gathers[after].third()
+        if before is not None:
+            reduce_second(before)
+        down(k, 0, dn // 2)
+        core_send(k, 0)
+        if before is not None:
+            reduce_third(before)
+        down(k, dn // 2, dn)
+        core_send(k, 1)
+    reduce_first(turn[3])
+    reduce_second(turn[3])
+    reduce_third(turn[3])
+    result = hid[...] + expert_weight(z) * fin[0].astype(F32)
+    for k in (1, 3, 2):
+        arrived(z_in.at[k], rs_s.at[k, 7], rs_r.at[k, 7], (z, d))
+        result = result + expert_weight(grp_of(k)) * z_in[k].astype(F32)
+    out[...] = result.astype(BF16)
+    for copy in sent:
+        copy.wait_send()
+
+    @pl.when(z < 3)
+    def _():
+        for c in range(pieces):
+            state_copy(c).wait_send()
+
+
+def fused(
+    ssm_input, gate_input, step_size, decay_rate, in_coeff, out_coeff, skip_gain, norm_gain,
+    out_proj, residual, ffn_gain, router, routes, gate_weight, up_weight, down_weight,
+):
+    rows, chans = ssm_input.shape
+    tok, dim = residual.shape
+    units = gate_weight.shape[2]
+    n_state = in_coeff.shape[1]
+    cols = out_proj.shape[1]
+    half = dim // 2
+    in_vmem = pl.BlockSpec(memory_space=pltpu.VMEM)
+    in_hbm = pl.BlockSpec(memory_space=pl.ANY)
+    dma = pltpu.SemaphoreType.DMA
+    return pl.pallas_call(
+        fused_kernel,
+        out_shape=jax.ShapeDtypeStruct((tok, dim), BF16),
+        in_specs=[in_vmem] * 12 + [in_hbm] * 4,
+        out_specs=in_vmem,
+        scratch_shapes=[
+            pltpu.VMEM(out_proj.shape, BF16),
+            pltpu.VMEM((dim, units), BF16),
+            pltpu.VMEM((dim, units), BF16),
+            pltpu.VMEM((units, dim), BF16),
+            pltpu.VMEM((n_state, chans), F32),
+            pltpu.VMEM((4, n_state, chans // 4), BF16),
+            pltpu.VMEM((4, n_state, chans // 4), BF16),
+            pltpu.VMEM((rows, chans), F32),
+            pltpu.VMEM((8, rows, chans), BF16),
+            pltpu.VMEM((rows, 128), F32),
+            pltpu.VMEM((8, tok, 128), F32),
+            pltpu.VMEM((rows, cols), BF16),
+            pltpu.VMEM((8, tok, cols), BF16),
+            pltpu.VMEM((tok, dim), F32),
+            pltpu.VMEM((4, 8 * tok, dim), BF16),
+            pltpu.VMEM((8 * tok, units), BF16),
+            pltpu.VMEM((4, 8 * tok, dim), BF16),
+            pltpu.VMEM((4, 4 * tok, dim), BF16),
+            pltpu.VMEM((4, 4 * tok, dim), BF16),
+            pltpu.VMEM((4, 2 * tok, half), BF16),
+            pltpu.VMEM((4, 2 * tok, half), BF16),
+            pltpu.VMEM((4, 2, tok, half), BF16),
+            pltpu.VMEM((4, tok, half), BF16),
+            pltpu.VMEM((4, tok, half), BF16),
+            pltpu.VMEM((4, tok, dim), BF16),
+            pltpu.VMEM((4, tok, dim), BF16),
+            dma((4,)),
+            dma((4,)),
+            dma((4,)),
+            dma((5, 8)),
+            dma((5, 8)),
+            dma((8,)),
+            dma((8,)),
+            dma((8,)),
+            dma((8,)),
+            dma((4,)),
+            dma((4,)),
+            dma((4, 8)),
+            dma((4, 8)),
+        ],
+        compiler_params=pltpu.CompilerParams(
+            collective_id=0, has_side_effects=True, vmem_limit_bytes=56 * 1024 * 1024
+        ),
+    )(
+        ssm_input, gate_input, step_size, decay_rate[None], in_coeff, out_coeff, skip_gain[None],
+        norm_gain[None], residual, ffn_gain[None], router, routes,
+        out_proj, gate_weight, up_weight, down_weight,
+    )
+
+
 def solution(mesh):
     placed = (
         P("grp", "dev"),
@@ -163,6 +639,7 @@
         P("grp", None, "dev"),
         P("grp", "dev", None),
     )
+    small = mesh.shape["grp"] == 4 and mesh.shape["dev"] == 8
     return jax.shard_map(
-        shards, mesh=mesh, in_specs=placed, out_specs=P(("grp", "dev"), None), check_vma=False
-    )
+        fused if small else shards, mesh=mesh, in_specs=placed, out_specs=P(("grp", "dev"), None), check_vma=False
+    )

time: 248 us -> 114 us (0.46)
  waiting for transfers between devices: 130 us -> 0 us
  Pallas kernels: 0 us -> 107 us
  blocking collectives: 58 us -> 0 us
  matrix products: 30 us -> 0 us
  between operations: 13.4 us -> 0.01 us
  starting transfers between devices: 8.22 us -> 0 us
  other arithmetic: 4.5 us -> 0 us
  local copies, waits for them, and re-layouts: 2.95 us -> 6.53 us
    pallas_call x0 -> x1, Pallas kernels: none -> 107 us  [fused(): pl.pallas_call(fused_kernel, out_shape=jax.ShapeDtypeStruct((tok, dim), B...]
    all_gather x2 -> x0, waiting for transfers between devices: 59 us -> none  [the longest x1 34 us: shards(): lax.all_gather(arrived, 'dev', axis=0, tiled=True).reshape(-1, model_dim)]
    reduce_scatter x1 -> x0, waiting for transfers between devices: 51.5 us -> none  [shards(): lax.psum_scatter(jnp.dot(hidden, down_weight[0], preferred_element_type=j...]
    dot_general x12 -> x0, matrix products: 30 us -> none  [the longest x1 7.65 us: shards(): up_act = jnp.dot(all_rows, up_weight[0], preferred_element_type=jnp.float32)]
    all_gather x2 -> x0, blocking collectives: 27.3 us -> none  [the longest x1 14.8 us: shards(): lax.all_gather(own_state[None].astype(jnp.bfloat16), 'grp', axis=0, tiled...]
    all_to_all x2 -> x0, waiting for transfers between devices: 19.4 us -> none  [the longest x1 14.1 us: shards(): lax.all_to_all(summed.reshape(experts, slot_cap, model_dim), 'grp', split...]
    all_to_all x1 -> x0, blocking collectives: 18.8 us -> none  [shards(): lax.all_to_all(outgoing, 'grp', split_axis=0, concat_axis=0, tiled=True)]
    psum x1 -> x0, blocking collectives: 11.8 us -> none  [shards(): squares = lax.psum(jnp.sum(gated_out * gated_out, axis=1), 'dev')]
  transfers between devices with their start and end apart: 5 -> 0, of which waited for: 5 -> 0; matrix products, arithmetic and copies ran while one was open for 0% -> 0% of each run, Pallas kernels for 0% -> 0%
where the time goes in v1:
time: 114 us; the launch traced here: 113 us
  Pallas kernels  107 us (94%)
  local copies, waits for them, and re-layouts  6.53 us (6%)
    pallas_call x1, Pallas kernels, fused(): pl.pallas_call(fused_kernel, out_shape=jax.ShapeDtypeStruct((tok, dim), B...  107 us
    unnamed x4, local copies, waits for them, and re-layouts  6.53 us

profile of v1, /device:TPU:0, one launch (start us, length us, event | category | flops | bytes accessed | tf_op | source)
XLA Modules:
  0.0 113.4 jit_solution(16975819836487426602)
XLA Ops:
  0.0 1.4 %copy.19.routes = s32[32,2]{1,0:T(8,128)} copy(s32[32,2]{0,1:T(2,128)} %param.28) | data formatting | bytes 512 | tf_op args[12]
  1.4 1.5 %copy.17.step = f32[256,8]{1,0:T(8,128)} copy(f32[256,8]{0,1:T(8,128)} %param.18) | data formatting | bytes 16384 | tf_op args[2]
  2.8 2.1 %copy.18.router = f32[2048,4]{1,0:T(8,128)} copy(f32[2048,4]{0,1:T(4,128)} %param.27) | data formatting | bytes 65536 | tf_op args[11]
  5.0 106.8 %shard_map.154 = bf16[32,2048]{1,0:T(8,128)(2,1)} custom-call(bf16[256,512]{1,0:T(8,128)(2,1)} %ssm.1, bf16[256,512]{1,0:T(8,128)(2,1)} %gate.1, f32[256,8]{1,0:T(8,128)} %copy.17.step, f32[1,8]{1,0:T(1,128)} %bitcast.6, bf16[256,128]{1,0:T(8,128)(2,1)} %in_c.1, bf16[256,128]{1,0:T(8,128)(2,1)} %out_c.1, f32[1,8]{1,0:T(1,128)} %bitcast.7, f32[1,512]{1,0:T(1,128)} %bitcast.5, ...), custom_call_target="tpu_custom_call" | custom-call | tf_op jit(solution)/shard_map/pallas_call | solution.py:567
  111.8 1.6 %copy.21 = bf16[32,2048]{1,0:T(8,128)(2,1)} copy(bf16[32,2048]{1,0:T(8,128)(2,1)} %shard_map.154) | data formatting | bytes 262144

commit v2 on v1

--- a/solution.py
+++ b/solution.py
@@ -167,7 +167,7 @@
 ):
     z, d = lax.axis_index("grp"), lax.axis_index("dev")
     rows, chans = ssm.shape
-    heads = step.shape[1]
+    heads = step.shape[0]
     width = chans // heads
     n_state = in_c.shape[1]
     tok, dim = res.shape
@@ -226,13 +226,21 @@
     def exact(a, b):
         return jnp.dot(a, b, precision=HIGHEST_PREC, preferred_element_type=F32)
 
+    def exact_t(a, b):
+        return lax.dot_general(
+            a, b, (((1,), (1,)), ((), ())), precision=HIGHEST_PREC, preferred_element_type=F32
+        )
+
     causal = iota((rows, rows), 0) >= iota((rows, rows), 1)
     pad = (iota((heads, 128), 0) == iota((heads, 128), 1)).astype(F32)
     expand = (iota((128, chans), 0) == lax.div(iota((128, chans), 1), width)).astype(F32)
-    log_pad = exact(-(step[...] * decay[...]), pad)
-    step_pad = exact(step[...], pad)
+    pad_t = (iota((128, heads), 0) == iota((128, heads), 1)).astype(F32)
+    decay_pad = exact(jnp.broadcast_to(decay[...], (8, heads)), pad)[0:1]
+    step_t = exact(pad_t, step[...])
+    step_pad = step_t.T
+    log_pad = -(step_pad * decay_pad)
     cum = exact(causal.astype(F32), log_pad)
-    cum_t, step_t = cum.T, step_pad.T
+    cum_t = cum.T
     cum_wide, step_wide = exact(cum, expand), exact(step_pad, expand)
     last = cum_wide[rows - 1 : rows]
     xf = ssm[...].astype(F32)
@@ -427,18 +435,21 @@
         gathers[k].first()
 
     gather_first(0)
-    logits = exact(x_all[0, 0:tok].astype(F32), router[...])
+    logits = exact_t(x_all[0, 0:tok].astype(F32), router[...])
+    same = (iota((tok, tok), 0) == iota((tok, tok), 1)).astype(F32)
+    named = exact_t(same, routes[...].astype(F32))
     experts = logits.shape[1]
-    ids = iota((tok, experts), 1)
-    named0, named1 = routes[:, 0:1] == ids, routes[:, 1:2] == ids
+    ids = iota((tok, experts), 1).astype(F32)
+    named0, named1 = jnp.abs(named[:, 0:1] - ids) < 0.5, jnp.abs(named[:, 1:2] - ids) < 0.5
     logit0 = jnp.sum(jnp.where(named0, logits, 0.0), axis=1, keepdims=True)
     logit1 = jnp.sum(jnp.where(named1, logits, 0.0), axis=1, keepdims=True)
     prob0 = 1.0 / (1.0 + jnp.exp(-(logit0 - logit1)))
     prob1 = 1.0 - prob0
 
     def expert_weight(e):
-        return jnp.where(routes[:, 0:1] == e, prob0, 0.0) + jnp.where(
-            routes[:, 1:2] == e, prob1, 0.0
+        e = jnp.full((tok, 1), e, jnp.int32).astype(F32)
+        return jnp.where(jnp.abs(named[:, 0:1] - e) < 0.5, prob0, 0.0) + jnp.where(
+            jnp.abs(named[:, 1:2] - e) < 0.5, prob1, 0.0
         )
 
     gathers[0].second()
@@ -521,20 +532,21 @@
             gathers[after].second()
         if n < 2:
             gather_first(turn[n + 2])
+        if n > 1:
+            reduce_third(turn[n - 2])
         if before is not None:
             reduce_first(before)
         gate_up(k, gu // 2, gu)
         if after is not None:
             gathers[after].third()
-        if before is not None:
-            reduce_second(before)
         down(k, 0, dn // 2)
         core_send(k, 0)
         if before is not None:
-            reduce_third(before)
+            reduce_second(before)
         down(k, dn // 2, dn)
         core_send(k, 1)
     reduce_first(turn[3])
+    reduce_third(turn[2])
     reduce_second(turn[3])
     reduce_third(turn[3])
     result = hid[...] + expert_weight(z) * fin[0].astype(F32)
@@ -614,8 +626,8 @@
             collective_id=0, has_side_effects=True, vmem_limit_bytes=56 * 1024 * 1024
         ),
     )(
-        ssm_input, gate_input, step_size, decay_rate[None], in_coeff, out_coeff, skip_gain[None],
-        norm_gain[None], residual, ffn_gain[None], router, routes,
+        ssm_input, gate_input, step_size.T, decay_rate[None], in_coeff, out_coeff, skip_gain[None],
+        norm_gain[None], residual, ffn_gain[None], router.T, routes.T,
         out_proj, gate_weight, up_weight, down_weight,
     )
 

time: 114 us -> 99.2 us (0.87)
  Pallas kernels: 107 us -> 97.5 us
  local copies, waits for them, and re-layouts: 6.53 us -> 1.57 us
    pallas_call x1, Pallas kernels: 107 us -> 97.5 us  [fused(): pl.pallas_call(fused_kernel, out_shape=jax.ShapeDtypeStruct((tok, dim), B...]
    unnamed x4 -> x1, local copies, waits for them, and re-layouts: 6.53 us -> 1.57 us
where the time goes in v2:
time: 99.2 us; the launch traced here: 99.1 us
  Pallas kernels  97.5 us (98%)
  local copies, waits for them, and re-layouts  1.57 us (2%)
    pallas_call x1, Pallas kernels, fused(): pl.pallas_call(fused_kernel, out_shape=jax.ShapeDtypeStruct((tok, dim), B...  97.5 us

profile of v2, /device:TPU:0, one launch (start us, length us, event | category | flops | bytes accessed | tf_op | source)
XLA Modules:
  0.0 99.1 jit_solution(12530301621363377551)
XLA Ops:
  0.0 97.5 %shard_map.154 = bf16[32,2048]{1,0:T(8,128)(2,1)} custom-call(bf16[256,512]{1,0:T(8,128)(2,1)} %ssm.1, bf16[256,512]{1,0:T(8,128)(2,1)} %gate.1, f32[8,256]{1,0:T(8,128)} %bitcast.8, f32[1,8]{1,0:T(1,128)} %bitcast.12, bf16[256,128]{1,0:T(8,128)(2,1)} %in_c.1, bf16[256,128]{1,0:T(8,128)(2,1)} %out_c.1, f32[1,8]{1,0:T(1,128)} %bitcast.13, f32[1,512]{1,0:T(1,128)} %bitcast.10, ...), custom_call_target="tpu_custom_call" | custom-call | tf_op jit(solution)/shard_map/pallas_call | solution.py:579
  97.5 1.6 %copy.18 = bf16[32,2048]{1,0:T(8,128)(2,1)} copy(bf16[32,2048]{1,0:T(8,128)(2,1)} %shard_map.154) | data formatting | bytes 262144
